TPU v7x, 32 devices: a whole 2x2x4 slice. The times are simulated.
32 devices in a mesh: dp: 16 (over z, x, core), blk: 2 (over y).
Axes of the slice: x: 2, y: 2, z: 4, core: 2. Of those that a mesh axis runs over, the one named last changes fastest.
Arguments:
- train_act: bfloat16 [128, 4096], P(('dp', 'blk')), may hold values from -3 to 3
- train_grad: bfloat16 [128, 8192], P(('dp', 'blk')), may hold values from -3 to 3
- query_act: bfloat16 [64, 4096], P('dp', 'blk'), may hold values from -3 to 3
- query_grad: bfloat16 [64, 8192], P('dp'), may hold values from -3 to 3
- act_basis: bfloat16 [4096, 512], P('blk'), may hold values from -0.25 to 0.25
- grad_basis: bfloat16 [512, 8192], P(None, 'dp'), may hold values from -0.25 to 0.25
- eigenvalues: float32 [4096, 8192], P('blk', 'dp'), may hold values from 0.05 to 5
- example_ids: int32 [128], replicated, may hold values from 0 to 31, never falling along the last dimension, each value on 1 to 12 neighbouring positions
- query_ids: int32 [64], replicated, may hold values from 0 to 15, never falling along the last dimension, each value on 1 to 12 neighbouring positions
Outputs:
- influence: float32 [32, 16], P('dp')
Inputs may be any that keep to these rules, and one draw needn't show every extreme that they name: `example_ids`: the tokens of one training example are contiguous and ids never fall; every example has a token. `query_ids`: the tokens of one query are contiguous and ids never fall; every query has a token.
All inputs are finite; a program needn't handle non-finite values.
Results may differ from a plain program's by a relative error of at most 0.0007.
The roundings to bfloat16 on the way count: a program that leaves them out, or rounds other values in their place, can miss the bound.
Values may be sent and summed in bfloat16 or wider, within the bound.
A program may use at most 64 MiB of HBM per device.

v0:
```python
import jax
import jax.numpy as jnp
from jax import lax
from jax.sharding import PartitionSpec as P

D = 4096
FF = 8192
QUERIES = 16
EX_DP = 2


def as_sent(x):

    def short(part):
        return part.astype(jnp.bfloat16) if part.dtype == jnp.float32 else part

    return jax.tree.map(short, x)


def partner(block, axis, stride):
    count = lax.axis_size(axis)
    route = []
    for low in range(count):
        high = low | 1 << stride
        if high != low and high < count:
            route += [(low, high), (high, low)]
    return lax.ppermute(block, axis, route)


def rotate_blocks(row_data, basis):
    row_count = row_data.shape[0]
    block_size = basis.shape[1]
    count_blocks = basis.shape[0] // block_size
    turned = jnp.einsum(
        "tnk,nkl->tnl",
        row_data.reshape(row_count, count_blocks, block_size),
        basis.reshape(count_blocks, block_size, block_size),
        preferred_element_type=jnp.float32,
    )
    return turned.reshape(row_count, count_blocks * block_size).astype(jnp.bfloat16)


def rotate_columns(row_data, basis):
    row_count = row_data.shape[0]
    full_width = row_data.shape[1]
    block_size = basis.shape[0]
    col_width = basis.shape[1]
    count_blocks = full_width // block_size
    turned = jnp.einsum(
        "tmk,kml->tml",
        row_data.reshape(row_count, count_blocks, block_size),
        basis.reshape(block_size, count_blocks, col_width // count_blocks),
        preferred_element_type=jnp.float32,
    )
    return turned.reshape(row_count, col_width).astype(jnp.bfloat16)


def join_pair(mine, other, is_upper):
    return jnp.where(is_upper, jnp.concatenate([other, mine], 1), jnp.concatenate([mine, other], 1))


def shards(
    train_act,
    train_grad,
    query_act,
    query_grad,
    act_basis,
    grad_basis,
    eigenvalues,
    example_ids,
    query_ids,
):
    devices_dp = lax.axis_size("dp")
    block_size = grad_basis.shape[0]
    col_width = grad_basis.shape[1]
    owned_width = act_basis.shape[0]
    eigen_sum = lax.psum(jnp.sum(eigenvalues), ("dp", "blk"))
    damping = 0.1 * eigen_sum / (D * FF)
    owned_rows = lax.all_to_all(train_act, "blk", split_axis=1, concat_axis=0, tiled=True)
    query_all = lax.all_gather(rotate_blocks(query_act, act_basis), "dp", axis=0, tiled=True)
    train_cols, query_cols = (
        lax.all_to_all(train_grad, "dp", split_axis=1, concat_axis=0, tiled=True),
        lax.all_to_all(query_grad, "dp", split_axis=1, concat_axis=0, tiled=True),
    )
    if col_width < block_size:
        position = lax.axis_index("dp")
        for bit_index in range((block_size // col_width).bit_length() - 1):
            other_train, other_query = (
                partner(as_sent(train_cols), "dp", bit_index).astype(train_cols.dtype),
                partner(as_sent(query_cols), "dp", bit_index).astype(query_cols.dtype),
            )
            is_upper = position >> bit_index & 1 == 1
            train_cols = join_pair(train_cols, other_train, is_upper)
            query_cols = join_pair(query_cols, other_query, is_upper)
    grad_mine = rotate_columns(train_cols, grad_basis)
    query_grad_rot = rotate_columns(query_cols, grad_basis)
    grad_all = lax.all_gather(
        grad_mine.reshape(devices_dp, 1, grad_mine.shape[0] // devices_dp, col_width),
        "blk",
        axis=1,
        tiled=True,
    )
    grad_all = grad_all.reshape(
        grad_all.shape[0] * grad_all.shape[1] * grad_all.shape[2], col_width
    )
    one_query = (query_ids[:, None] == jnp.arange(QUERIES, dtype=jnp.int32)[None, :]).astype(
        jnp.bfloat16
    )
    weighted = one_query.T[:, :, None] * query_all[None, :, :]
    query_gram = jnp.einsum(
        "qti,tj->iqj", weighted, query_grad_rot, preferred_element_type=jnp.float32
    )
    norm_scale = float(D * FF) ** (-0.5)
    precond = (query_gram / (eigenvalues[:, None, :] + damping) * norm_scale).astype(jnp.bfloat16)
    precond = precond.reshape(owned_width, QUERIES * col_width)
    shard_rows = lax.all_gather(rotate_blocks(owned_rows, act_basis), "dp", axis=0, tiled=True)
    row_count = shard_rows.shape[0]
    mixed_rows = jnp.dot(shard_rows, precond, preferred_element_type=jnp.float32).reshape(
        row_count, QUERIES, col_width
    )
    token_score = jnp.sum(mixed_rows * grad_all[:, None, :].astype(jnp.float32), axis=2)
    example_count = EX_DP * devices_dp
    one_example = (
        example_ids[:, None] == jnp.arange(example_count, dtype=jnp.int32)[None, :]
    ).astype(jnp.float32)
    partial_scores = jnp.dot(one_example.T, token_score, precision=lax.Precision.HIGHEST)
    all_scores = lax.psum(partial_scores, ("dp", "blk"))
    return lax.dynamic_slice_in_dim(all_scores, lax.axis_index("dp") * EX_DP, EX_DP, 0)


def solution(mesh):
    placed = (
        P(("dp", "blk"), None),
        P(("dp", "blk"), None),
        P("dp", "blk"),
        P("dp", None),
        P("blk", None),
        P(None, "dp"),
        P("blk", "dp"),
        P(),
        P(),
    )
    return jax.shard_map(
        shards, mesh=mesh, in_specs=placed, out_specs=P("dp", None), check_vma=False
    )
```

profile of v0, /device:TPU:0, one launch (start us, length us, event | category | flops | bytes accessed | tf_op | source)
XLA Modules:
  0.0 184.5 jit_solution(16810022378639869197)
XLA Ops:
  0.0 4.0 %reduce_sum.18 = f32[]{:T(128)} reduce(f32[2048,512]{1,0:T(8,128)} %param.15, f32[]{:T(128)} %constant.8.clone.1), dimensions={0,1}, to_apply=%region_0.0 | reduce | flops 1048575 | bytes 4194312 | tf_op jit(solution)/shard_map/reduce_sum | solution.py:77
  4.0 4.2 %all-to-all-start = ((bf16[4,2,2048]{2,0,1:T(4,128)(2,1)}), bf16[4,2,2048]{2,0,1:T(4,128)(2,1)S(1)}, u32[]{:S(2)}, u32[]{:S(2)}) async-start(bf16[4,2,2048]{2,0,1:T(4,128)(2,1)} %bitcast.1), calls=%async_computation | async-start | bytes 65536 | tf_op jit(solution)/shard_map/all_to_all | solution.py:79
  8.3 41.7 %psum.14 = f32[]{:T(128)} all-reduce(f32[]{:T(128)} %reduce_sum.18), channel_id=1, replica_groups=mesh['dp'=16,'blk'=2] {'dp','blk'}, use_global_device_ids=true, to_apply=%region_1.0 | all-reduce | flops 1 | bytes 8 | tf_op jit(solution)/shard_map/psum | solution.py:77
  50.6 0.0 copy-start.3
  50.6 0.0 copy-start.2
  50.7 4.7 %broadcast_add_fusion = f32[2048,512]{1,0:T(8,128)} fusion(f32[2048,512]{1,0:T(8,128)} %param.15, f32[]{:T(128)S(6)} %div.11), kind=kLoop, calls=%fused_computation.8 | loop fusion | flops 1048576 | bytes 8388612 | tf_op jit(solution)/shard_map/add | solution.py:114
  55.3 0.4 convolution_convert_fusion.3
  55.7 21.7 %all-gather = bf16[16,4,2048]{2,1,0:T(4,128)(2,1)S(1)} all-gather(bf16[1,4,2048]{2,1,0:T(4,128)(2,1)S(1)} %bitcast.67), channel_id=1, replica_groups=mesh['dp'=16,'blk'=2] {'dp'}, dimensions={0}, use_global_device_ids=true | all-gather | bytes 278528 | tf_op jit(solution)/shard_map/all_gather | solution.py:80
  77.4 5.4 %copy.30 = f32[2048,512]{0,1:T(8,128)} copy(f32[2048,512]{1,0:T(8,128)} %broadcast_add_fusion) | data formatting | bytes 8388608 | tf_op jit(solution)/shard_map/add | solution.py:114
  82.9 0.8 reshape.106
  83.6 3.5 %all-to-all-start.2 = ((bf16[4,16,512]{2,0,1:T(4,128)(2,1)}), bf16[4,16,512]{2,0,1:T(4,128)(2,1)S(1)}, u32[]{:S(2)}, u32[]{:S(2)}) async-start(bf16[4,16,512]{2,0,1:T(4,128)(2,1)} %bitcast.19), calls=%async_computation.2 | async-start | bytes 131072 | tf_op jit(solution)/shard_map/all_to_all | solution.py:82
  87.2 0.4 convolution_convert_fusion.2
  87.5 23.2 %all_gather.9 = bf16[128,2048]{1,0:T(8,128)(2,1)S(1)} all-gather(bf16[8,2048]{1,0:T(8,128)(2,1)S(1)} %bitcast.65), channel_id=1, replica_groups=mesh['dp'=16,'blk'=2] {'dp'}, dimensions={0}, use_global_device_ids=true | all-gather | bytes 557056 | tf_op jit(solution)/shard_map/all_gather | solution.py:116
  110.7 4.2 %all-to-all-start.1 = ((bf16[4,16,512]{2,0,1:T(4,128)(2,1)}), bf16[4,16,512]{2,0,1:T(4,128)(2,1)}, u32[]{:S(2)}, u32[]{:S(2)}) async-start(bf16[4,16,512]{2,0,1:T(4,128)(2,1)} %bitcast.6), calls=%async_computation.1 | async-start | bytes 131072 | tf_op jit(solution)/shard_map/all_to_all | solution.py:83
  114.9 0.2 fusion.14
  115.2 4.9 %all_gather.11 = bf16[16,2,4,512]{3,2,1,0:T(4,128)(2,1)S(1)} all-gather(bf16[16,1,4,512]{3,2,1,0:T(4,128)(2,1)S(1)} %bitcast.63), channel_id=1, replica_groups=mesh['dp'=16,'blk'=2] {'blk'}, dimensions={1}, use_global_device_ids=true | all-gather | bytes 196608 | tf_op jit(solution)/shard_map/all_gather | solution.py:97
  120.1 1.7 all-to-all-done.1
  121.8 0.9 reshape.100
  122.7 0.2 fusion.13
  122.9 0.0 copy-start.4
  122.9 22.5 %multiply_reduce_fusion = f32[128,16]{0,1:T(8,128)S(1)} fusion(f32[128,512]{1,0:T(8,128)S(1)} %reshape.104, f32[2048,512]{0,1:T(8,128)} %copy.30, bf16[64,512,1]{1,0,2:T(8,128)(2,1)S(1)} %fusion.13, bf16[64,2048]{1,0:T(8,128)(2,1)} %reshape.106, bf16[16,64]{1,0:T(8,128)(2,1)S(1)} %fusion.25, bf16[128,2048]{1,0:T(8,128)(2,1)S(1)} %all_gather.9), kind=kOutput, calls=%fused_computation.6 | convolution fusion | flops 6503266304 | bytes 5318656 | tf_op jit(solution)/shard_map/dot_general | solution.py:118
  145.4 0.2 fusion.21
  145.7 38.2 %psum.15 = f32[32,16]{1,0:T(8,128)S(1)} all-reduce(f32[32,16]{1,0:T(8,128)S(1)} %fusion.21), channel_id=1, replica_groups=mesh['dp'=16,'blk'=2] {'dp','blk'}, use_global_device_ids=true, to_apply=%region_3.0 | all-reduce | flops 512 | bytes 4096 | tf_op jit(solution)/shard_map/psum | solution.py:127
  183.9 0.6 constant_dynamic-slice_fusion
  (14 shorter events, 0.1 us)
Async XLA Ops:
  0.0 55.3 %copy-start = (bf16[2048,512]{1,0:T(8,128)(2,1)S(1)}, bf16[2048,512]{1,0:T(8,128)(2,1)}, u32[]{:S(2)}) copy-start(bf16[2048,512]{1,0:T(8,128)(2,1)} %param.13) | copy-start | bytes 6291460
  4.0 79.6 %all-to-all-start = ((bf16[4,2,2048]{2,0,1:T(4,128)(2,1)}), bf16[4,2,2048]{2,0,1:T(4,128)(2,1)S(1)}, u32[]{:S(2)}, u32[]{:S(2)}) async-start(bf16[4,2,2048]{2,0,1:T(4,128)(2,1)} %bitcast.1), calls=%async_computation | async-start | bytes 65536 | tf_op jit(solution)/shard_map/all_to_all | solution.py:79
  50.6 4.7 %copy-start.3 = (s32[64]{0:T(128)S(1)}, s32[64]{0:T(128)}, u32[]{:S(2)}) copy-start(s32[64]{0:T(128)} %param.17) | copy-start | bytes 772
  50.6 4.7 %copy-start.2 = (bf16[4,2048]{1,0:T(4,128)(2,1)S(1)}, bf16[4,2048]{1,0:T(4,128)(2,1)}, u32[]{:S(2)}) copy-start(bf16[4,2048]{1,0:T(4,128)(2,1)} %param.11) | copy-start | bytes 49156
  77.4 37.5 %copy-start.1 = (bf16[512,512]{1,0:T(8,128)(2,1)S(1)}, bf16[512,512]{1,0:T(8,128)(2,1)}, u32[]{:S(2)}) copy-start(bf16[512,512]{1,0:T(8,128)(2,1)} %param.14) | copy-start | bytes 1572868
  83.6 27.1 %all-to-all-start.2 = ((bf16[4,16,512]{2,0,1:T(4,128)(2,1)}), bf16[4,16,512]{2,0,1:T(4,128)(2,1)S(1)}, u32[]{:S(2)}, u32[]{:S(2)}) async-start(bf16[4,16,512]{2,0,1:T(4,128)(2,1)} %bitcast.19), calls=%async_computation.2 | async-start | bytes 131072 | tf_op jit(solution)/shard_map/all_to_all | solution.py:82
  110.7 11.1 %all-to-all-start.1 = ((bf16[4,16,512]{2,0,1:T(4,128)(2,1)}), bf16[4,16,512]{2,0,1:T(4,128)(2,1)}, u32[]{:S(2)}, u32[]{:S(2)}) async-start(bf16[4,16,512]{2,0,1:T(4,128)(2,1)} %bitcast.6), calls=%async_computation.1 | async-start | bytes 131072 | tf_op jit(solution)/shard_map/all_to_all | solution.py:83
  122.9 22.6 %copy-start.4 = (s32[128]{0:T(128)S(1)}, s32[128]{0:T(128)}, u32[]{:S(2)}) copy-start(s32[128]{0:T(128)} %param.16) | copy-start | bytes 1540
where the time goes:
time: 185 us; the launch traced here: 184 us
  blocking collectives  130 us (70%)
  matrix products  23.9 us (13%)
  starting transfers between devices  11.9 us (6%)
  other arithmetic  8.68 us (5%)
  local copies, waits for them, and re-layouts  7.72 us (4%)
    psum x1, blocking collectives, shards(): eigen_sum = lax.psum(jnp.sum(eigenvalues), ('dp', 'blk'))  41.7 us
    psum x1, blocking collectives, shards(): all_scores = lax.psum(partial_scores, ('dp', 'blk'))  38.2 us
    all_gather x1, blocking collectives, shards(): lax.all_gather(rotate_blocks(owned_rows, act_basis), 'dp', axis=0, tiled=...  23.2 us
    dot_general x1, matrix products, shards(): jnp.dot(shard_rows, precond, preferred_element_type=jnp.float32)  22.5 us
    all_gather x1, blocking collectives, shards(): lax.all_gather(rotate_blocks(query_act, act_basis), 'dp', axis=0, tiled=T...  21.7 us
    add x1, local copies, waits for them, and re-layouts, shards(): eigenvalues[:, None, :] + damping  5.43 us
    all_gather x1, blocking collectives, shards(): lax.all_gather(grad_mine.reshape(devices_dp, 1, grad_mine.shape[0] // dev...  4.94 us
    add x1, other arithmetic, shards(): eigenvalues[:, None, :] + damping  4.66 us
  transfers between devices with their start and end apart: 3, of which 1 were waited for; matrix products, arithmetic and copies ran while one was open for 6% of the time, Pallas kernels for 0%

commit v1 on v0

--- a/solution.py
+++ b/solution.py
@@ -1,12 +1,328 @@
+import functools
+
 import jax
 import jax.numpy as jnp
 from jax import lax
+from jax.experimental import pallas as pl
+from jax.experimental.pallas import tpu as pltpu
 from jax.sharding import PartitionSpec as P
 
 D = 4096
 FF = 8192
 QUERIES = 16
 EX_DP = 2
+MESH = pl.DeviceIdType.MESH
+VMEM = pl.BlockSpec(memory_space=pltpu.VMEM)
+ANY = pl.BlockSpec(memory_space=pl.ANY)
+
+
+def greet_all(ndp, nblk, me):
+    count = ndp * nblk
+    barrier = pltpu.get_barrier_semaphore()
+
+    @pl.loop(1, count)
+    def _(k):
+        to = lax.rem(me + k, count)
+        pl.semaphore_signal(
+            barrier, inc=1, device_id=(to // nblk, lax.rem(to, nblk)), device_id_type=MESH
+        )
+
+    pl.semaphore_wait(barrier, count - 1)
+
+
+def exchange_kernel(
+    ndp, nblk, ta, tg, qa, qg, eig, ta_o, tg_o, qa_o, qg_o, parts,
+    eig_v, part, eig_sem, s_ta, s_tg, s_qa, s_qg, s_eig, r_sem, swap_s, swap_r,
+):
+    dp, blk = lax.axis_index("dp"), lax.axis_index("blk")
+    half, core = dp // 2, lax.rem(dp, 2)
+    me = dp * nblk + blk
+    count = ndp * nblk
+    nh = ndp // 2
+    wa = qa.shape[1]
+    wg = tg_o.shape[-1]
+    load = pltpu.make_async_copy(eig, eig_v, eig_sem)
+    load.start()
+    greet_all(ndp, nblk, me)
+
+    def put_ta(k):
+        to = lax.rem(half * nblk + blk + k, nh * nblk)
+        h, b = to // nblk, lax.rem(to, nblk)
+        return pltpu.make_async_remote_copy(
+            ta.at[:, pl.ds(pl.multiple_of(b * wa, 128), wa)], ta_o.at[half, core, blk],
+            s_ta.at[k], r_sem.at[0], device_id=(h * 2 + core, b), device_id_type=MESH)
+
+    def put_qa(k):
+        h = lax.rem(half + k, nh)
+        return pltpu.make_async_remote_copy(
+            qa, qa_o.at[half, core], s_qa.at[k], r_sem.at[1],
+            device_id=(h * 2 + core, blk), device_id_type=MESH)
+
+    def put_tg(k):
+        to = lax.rem(me + k, count)
+        d, b = to // nblk, lax.rem(to, nblk)
+        return pltpu.make_async_remote_copy(
+            tg.at[:, pl.ds(pl.multiple_of(d * wg, 128), wg)], tg_o.at[me],
+            s_tg.at[k], r_sem.at[2], device_id=(d, b), device_id_type=MESH)
+
+    def put_qg(k):
+        d = lax.rem(dp + k, ndp)
+        return pltpu.make_async_remote_copy(
+            qg.at[:, pl.ds(pl.multiple_of(d * wg, 128), wg)], qg_o.at[dp],
+            s_qg.at[k], r_sem.at[3], device_id=(d, blk), device_id_type=MESH)
+
+    def put_eig(k):
+        to = lax.rem(me + k, count)
+        return pltpu.make_async_remote_copy(
+            part, parts.at[me], s_eig.at[k], r_sem.at[4],
+            device_id=(to // nblk, lax.rem(to, nblk)), device_id_type=MESH)
+
+    @pl.loop(1, nh)
+    def _(k):
+        put_qa(k).start()
+
+    @pl.loop(1, nh * nblk)
+    def _(k):
+        put_ta(k).start()
+
+    pltpu.make_async_copy(
+        ta.at[:, pl.ds(pl.multiple_of(blk * wa, 128), wa)], ta_o.at[half, core, blk], r_sem.at[0]
+    ).start()
+    pltpu.make_async_copy(qa, qa_o.at[half, core], r_sem.at[1]).start()
+    mine = pl.ds(pl.multiple_of(dp * wg, 128), wg)
+    pltpu.make_async_copy(tg.at[:, mine], tg_o.at[me], r_sem.at[2]).start()
+    pltpu.make_async_copy(qg.at[:, mine], qg_o.at[dp], r_sem.at[3]).start()
+
+    load.wait()
+    rows = eig_v.shape[0]
+    total = jnp.zeros((8, eig_v.shape[1]), jnp.float32)
+
+    def add(i, total):
+        block = eig_v[pl.ds(pl.multiple_of(i * 256, 256), 256), :]
+        return total + jnp.sum(block.reshape(32, 8, block.shape[1]), axis=0)
+
+    total = lax.fori_loop(0, rows // 256, add, total)
+    lanes = total[:, 0:128]
+    for c in range(1, eig_v.shape[1] // 128):
+        lanes = lanes + total[:, c * 128:(c + 1) * 128]
+    part[...] = lanes
+
+    @pl.loop(1, count)
+    def _(k):
+        put_eig(k).start()
+
+    pltpu.make_async_copy(part, parts.at[me], r_sem.at[4]).start()
+
+    @pl.loop(1, ndp)
+    def _(k):
+        put_qg(k).start()
+
+    @pl.loop(1, count)
+    def _(k):
+        put_tg(k).start()
+
+    def swap(buf, at):
+        return pltpu.make_async_remote_copy(
+            buf.at[:, core], buf.at[:, core], swap_s.at[at], swap_r.at[at],
+            device_id=(half * 2 + 1 - core, blk), device_id_type=MESH)
+
+    pltpu.make_async_copy(qa_o.at[:, core], qa_o.at[:, core], r_sem.at[1]).wait()
+    swap_q = swap(qa_o, 0)
+    swap_q.start()
+    pltpu.make_async_copy(ta_o.at[:, core], ta_o.at[:, core], r_sem.at[0]).wait()
+    swap_t = swap(ta_o, 1)
+    swap_t.start()
+    pltpu.make_async_copy(parts, parts, r_sem.at[4]).wait()
+    pltpu.make_async_copy(qg_o, qg_o, r_sem.at[3]).wait()
+    pltpu.make_async_copy(tg_o, tg_o, r_sem.at[2]).wait()
+
+    @pl.loop(1, nh)
+    def _(k):
+        put_qa(k).wait_send()
+
+    @pl.loop(1, nh * nblk)
+    def _(k):
+        put_ta(k).wait_send()
+
+    @pl.loop(1, ndp)
+    def _(k):
+        put_qg(k).wait_send()
+
+    @pl.loop(1, count)
+    def _(k):
+        put_tg(k).wait_send()
+        put_eig(k).wait_send()
+
+    swap_q.wait()
+    swap_t.wait()
+
+
+def exchange(ndp, nblk, ta, tg, qa, qg, eig):
+    count = ndp * nblk
+    nh = ndp // 2
+    tok, qtok = ta.shape[0], qa.shape[0]
+    wa, wg = qa.shape[1], tg.shape[1] // ndp
+    bf = jnp.bfloat16
+    dma = pltpu.SemaphoreType.DMA
+    return pl.pallas_call(
+        functools.partial(exchange_kernel, ndp, nblk),
+        out_shape=(
+            jax.ShapeDtypeStruct((nh, 2, nblk, tok, wa), bf),
+            jax.ShapeDtypeStruct((count, tok, wg), bf),
+            jax.ShapeDtypeStruct((nh, 2, qtok, wa), bf),
+            jax.ShapeDtypeStruct((ndp, qtok, wg), bf),
+            jax.ShapeDtypeStruct((count, 8, 128), jnp.float32),
+        ),
+        in_specs=[VMEM, VMEM, VMEM, VMEM, ANY],
+        out_specs=(VMEM,) * 5,
+        scratch_shapes=[
+            pltpu.VMEM(eig.shape, jnp.float32),
+            pltpu.VMEM((8, 128), jnp.float32),
+            dma(()),
+            dma((nh * nblk,)), dma((count,)), dma((nh,)), dma((ndp,)), dma((count,)),
+            dma((5,)), dma((2,)), dma((2,)),
+        ],
+        compiler_params=pltpu.CompilerParams(
+            collective_id=0, has_side_effects=True, vmem_limit_bytes=32 * 2**20
+        ),
+        name="exchange",
+    )(ta, tg, qa, qg, eig)
+
+
+def score_kernel(
+    ta, tg, qa, qg, parts, act_basis, grad_basis, eig, qids, eids, out,
+    tf, gf, qf, qgf, act, grad, query_t, qgrad, weight, score,
+):
+    bf, f32 = jnp.bfloat16, jnp.float32
+    count, tok, wa = ta.shape
+    nq, qtok, wg = qg.shape
+    block = act_basis.shape[1]
+    tokens = count * tok
+    for s in range(count):
+        tf[s * tok:(s + 1) * tok, :] = ta[s].astype(f32)
+        gf[s * tok:(s + 1) * tok, :] = tg[s].astype(f32)
+    for s in range(nq):
+        qf[s * qtok:(s + 1) * qtok, :] = qa[s].astype(f32)
+        qgf[s * qtok:(s + 1) * qtok, :] = qg[s].astype(f32)
+    damping = 0.1 * jnp.sum(parts[...]) / (D * FF)
+    grad[...] = jnp.dot(
+        gf[...].astype(bf), grad_basis[...], preferred_element_type=f32).astype(bf).astype(f32)
+    qgrad[...] = jnp.dot(
+        qgf[...].astype(bf), grad_basis[...], preferred_element_type=f32).astype(bf)
+    score[...] = jnp.zeros_like(score)
+    norm_scale = float(D * FF) ** (-0.5)
+
+    @pl.loop(0, wa // block)
+    def _(n):
+        at = pl.ds(pl.multiple_of(n * block, block), block)
+        basis = act_basis[at, :]
+        act[...] = jnp.dot(
+            tf[:, at].astype(bf), basis, preferred_element_type=f32).astype(bf)
+        turned = jnp.dot(qf[:, at].astype(bf), basis, preferred_element_type=f32)
+        query_t[...] = turned.astype(bf).astype(f32).T.astype(bf)
+        weight[...] = norm_scale / (eig[at, :] + damping)
+
+        @pl.loop(0, QUERIES, unroll=2)
+        def _(q):
+            of_q = jnp.where(qids[...] == q, qgrad[...].astype(f32), 0.0).astype(bf)
+            gram = jnp.dot(query_t[...], of_q, preferred_element_type=f32)
+            precond = (gram * weight[...]).astype(bf)
+            mixed = jnp.dot(act[...], precond, preferred_element_type=f32) * grad[...]
+            total = mixed[:, 0:128]
+            for c in range(1, wg // 128):
+                total = total + mixed[:, c * 128:(c + 1) * 128]
+            score[q] += total
+
+    examples = out.shape[0] * out.shape[1]
+    one = (lax.broadcasted_iota(jnp.int32, (examples, tokens), 0) == eids[...]).astype(f32)
+    lane = lax.broadcasted_iota(jnp.int32, (examples, QUERIES), 1)
+    result = jnp.zeros((examples, QUERIES), f32)
+    for q in range(QUERIES):
+        of_ex = jnp.dot(one, score[q], precision=lax.Precision.HIGHEST, preferred_element_type=f32)
+        result = result + jnp.where(lane == q, jnp.sum(of_ex, axis=1, keepdims=True), 0.0)
+    for d in range(out.shape[0]):
+        out[d] = result[d * EX_DP:(d + 1) * EX_DP, :]
+
+
+def scores(ndp, ta, tg, qa, qg, parts, act_basis, grad_basis, eig, qids, eids):
+    count, tok, wa = ta.shape
+    nq, qtok, wg = qg.shape
+    block = act_basis.shape[1]
+    tokens, qtokens = count * tok, nq * qtok
+    bf, f32 = jnp.bfloat16, jnp.float32
+    return pl.pallas_call(
+        score_kernel,
+        out_shape=jax.ShapeDtypeStruct((ndp, EX_DP, QUERIES), f32),
+        in_specs=[VMEM] * 10,
+        out_specs=VMEM,
+        scratch_shapes=[
+            pltpu.VMEM((tokens, wa), f32), pltpu.VMEM((tokens, wg), f32),
+            pltpu.VMEM((qtokens, wa), f32), pltpu.VMEM((qtokens, wg), f32),
+            pltpu.VMEM((tokens, block), bf), pltpu.VMEM((tokens, wg), f32),
+            pltpu.VMEM((block, qtokens), bf), pltpu.VMEM((qtokens, wg), bf),
+            pltpu.VMEM((block, wg), f32), pltpu.VMEM((QUERIES, tokens, 128), f32),
+        ],
+        compiler_params=pltpu.CompilerParams(vmem_limit_bytes=48 * 2**20),
+        name="scores",
+    )(ta, tg, qa, qg, parts, act_basis, grad_basis, eig, qids, eids)
+
+
+def reduce_kernel(ndp, nblk, partial, out, slots, s_sem, r_sem):
+    dp, blk = lax.axis_index("dp"), lax.axis_index("blk")
+    me = dp * nblk + blk
+    count = ndp * nblk
+    greet_all(ndp, nblk, me)
+
+    def put(k):
+        to = lax.rem(me + k, count)
+        d = to // nblk
+        return pltpu.make_async_remote_copy(
+            partial.at[d], slots.at[me], s_sem.at[k], r_sem,
+            device_id=(d, lax.rem(to, nblk)), device_id_type=MESH)
+
+    @pl.loop(1, count)
+    def _(k):
+        put(k).start()
+
+    pltpu.make_async_copy(partial.at[dp], slots.at[me], r_sem).start()
+
+    @pl.loop(1, count)
+    def _(k):
+        put(k).wait_send()
+
+    pltpu.make_async_copy(slots, slots, r_sem).wait()
+    out[...] = jnp.sum(slots[...], axis=0)
+
+
+def reduce_scores(ndp, nblk, partial):
+    count = ndp * nblk
+    dma = pltpu.SemaphoreType.DMA
+    return pl.pallas_call(
+        functools.partial(reduce_kernel, ndp, nblk),
+        out_shape=jax.ShapeDtypeStruct(partial.shape[1:], jnp.float32),
+        in_specs=[VMEM],
+        out_specs=VMEM,
+        scratch_shapes=[
+            pltpu.VMEM((count,) + partial.shape[1:], jnp.float32), dma((count,)), dma(()),
+        ],
+        compiler_params=pltpu.CompilerParams(collective_id=1, has_side_effects=True),
+        name="reduce_scores",
+    )(partial)
+
+
+def shards_square(
+    train_act, train_grad, query_act, query_grad, act_basis, grad_basis, eigenvalues,
+    example_ids, query_ids,
+):
+    ndp, nblk = lax.axis_size("dp"), lax.axis_size("blk")
+    ta, tg, qa, qg, parts = exchange(
+        ndp, nblk, train_act, train_grad, query_act, query_grad, eigenvalues)
+    ta = ta.reshape((ndp * nblk,) + ta.shape[3:])
+    qa = qa.reshape((ndp,) + qa.shape[2:])
+    partial = scores(
+        ndp, ta, tg, qa, qg, parts, act_basis, grad_basis, eigenvalues,
+        query_ids[:, None], example_ids[None, :])
+    return reduce_scores(ndp, nblk, partial)
 
 
 def as_sent(x):
@@ -140,6 +456,13 @@
         P(),
         P(),
     )
-    return jax.shard_map(
-        shards, mesh=mesh, in_specs=placed, out_specs=P("dp", None), check_vma=False
-    )
+    ndp = mesh.shape["dp"]
+
+    def run(*arrays):
+        square = arrays[5].shape[0] * ndp == arrays[5].shape[1] and ndp % 2 == 0
+        return jax.shard_map(
+            shards_square if square else shards,
+            mesh=mesh, in_specs=placed, out_specs=P("dp", None), check_vma=False
+        )(*arrays)
+
+    return run

time: 185 us -> 75.2 us (0.41)
  blocking collectives: 130 us -> 0 us
  Pallas kernels: 0 us -> 66.8 us
  matrix products: 23.9 us -> 0 us
  starting transfers between devices: 11.9 us -> 0 us
  other arithmetic: 8.68 us -> 0 us
    psum x2 -> x0, blocking collectives: 79.9 us -> none  [the longest x1 41.7 us: shards(): eigen_sum = lax.psum(jnp.sum(eigenvalues), ('dp', 'blk'))]
    pallas_call x0 -> x3, Pallas kernels: none -> 66.8 us  [the longest x1 32.4 us: scores(): pl.pallas_call(score_kernel, out_shape=jax.ShapeDtypeStruct((ndp, EX_DP,...]
    all_gather x3 -> x0, blocking collectives: 49.9 us -> none  [the longest x1 23.2 us: shards(): lax.all_gather(rotate_blocks(owned_rows, act_basis), 'dp', axis=0, tiled=...]
    dot_general x6 -> x0, matrix products: 23.9 us -> none  [the longest x1 22.5 us: shards(): jnp.dot(shard_rows, precond, preferred_element_type=jnp.float32)]
    all_to_all x3 -> x0, starting transfers between devices: 11.9 us -> none  [the longest x1 4.23 us: shards(): lax.all_to_all(train_act, 'blk', split_axis=1, concat_axis=0, tiled=True)]
    unnamed x11 -> x19, local copies, waits for them, and re-layouts: 0.78 us -> 7.14 us
    add x1 -> x0, local copies, waits for them, and re-layouts: 5.43 us -> none  [shards(): eigenvalues[:, None, :] + damping]
    add x1 -> x0, other arithmetic: 4.66 us -> none  [shards(): eigenvalues[:, None, :] + damping]
  transfers between devices with their start and end apart: 3 -> 0, of which waited for: 1 -> 0; matrix products, arithmetic and copies ran while one was open for 6% -> 0% of each run, Pallas kernels for 0% -> 0%
where the time goes in v1:
time: 75.2 us; the launch traced here: 74.7 us
  Pallas kernels  66.8 us (89%)
  local copies, waits for them, and re-layouts  7.9 us (11%)
    pallas_call x1, Pallas kernels, scores(): pl.pallas_call(score_kernel, out_shape=jax.ShapeDtypeStruct((ndp, EX_DP,...  32.4 us
    pallas_call x1, Pallas kernels, exchange(): pl.pallas_call(functools.partial(exchange_kernel, ndp, nblk), out_shape=(...  25.1 us
    pallas_call x1, Pallas kernels, reduce_scores(): pl.pallas_call(functools.partial(reduce_kernel, ndp, nblk), out_shape=jax...  9.31 us
    unnamed x19, local copies, waits for them, and re-layouts  7.14 us

profile of v1, /device:TPU:0, one launch (start us, length us, event | category | flops | bytes accessed | tf_op | source)
XLA Modules:
  0.0 74.7 jit_solution(966476248755977543)
XLA Ops:
  0.0 0.0 copy-start.8
  0.0 0.8 %copy.10.qids = s32[64,1]{1,0:T(8,128)S(1)} copy(s32[64,1]{0,1:T(1,128)} %bitcast.7) | data formatting | bytes 512 | tf_op jit(solution)/shard_map/broadcast_in_dim | solution.py:324
  0.8 0.0 copy-start
  0.8 2.2 %copy-done = f32[2048,512]{1,0:T(8,128)S(1)} copy-done((f32[2048,512]{1,0:T(8,128)S(1)}, f32[2048,512]{1,0:T(8,128)}, u32[]{:S(2)}) %copy-start) | copy-done | bytes 4194328
  2.9 0.0 copy-start.3
  3.0 0.8 %copy-done.3 = bf16[4,8192]{1,0:T(4,128)(2,1)S(1)} copy-done((bf16[4,8192]{1,0:T(4,128)(2,1)S(1)}, bf16[4,8192]{1,0:T(4,128)(2,1)}, u32[]{:S(2)}) %copy-start.3) | copy-done | bytes 65560
  3.8 0.0 copy-start.4
  3.8 0.8 %copy-done.4 = bf16[4,8192]{1,0:T(4,128)(2,1)S(1)} copy-done((bf16[4,8192]{1,0:T(4,128)(2,1)S(1)}, bf16[4,8192]{1,0:T(4,128)(2,1)}, u32[]{:S(2)}) %copy-start.4) | copy-done | bytes 65560
  4.6 0.0 copy-start.6
  4.6 0.8 %copy-done.6 = bf16[4,4096]{1,0:T(4,128)(2,1)S(1)} copy-done((bf16[4,4096]{1,0:T(4,128)(2,1)S(1)}, bf16[4,4096]{1,0:T(4,128)(2,1)}, u32[]{:S(2)}) %copy-start.6) | copy-done | bytes 32792
  5.4 0.0 copy-start.7
  5.4 0.7 copy-done.7
  6.1 0.0 copy-start.1
  6.1 0.0 copy-start.2
  6.1 25.1 %exchange.1 = (bf16[8,2,2,4,2048]{4,3,2,1,0:T(4,128)(2,1)S(1)}, bf16[32,4,512]{2,1,0:T(4,128)(2,1)S(1)}, bf16[8,2,4,2048]{3,2,1,0:T(4,128)(2,1)S(1)}, bf16[16,4,512]{2,1,0:T(4,128)(2,1)S(1)}, f32[32,8,128]{2,1,0:T(8,128)S(1)}) custom-call(bf16[4,4096]{1,0:T(4,128)(2,1)S(1)} %copy-done.6, bf16[4,8192]{1,0:T(4,128)(2,1)S(1)} %copy-done.3, ...), custom_call_target="tpu_custom_call" | custom-call | tf_op jit(solution)/shard_map/exchange/pallas_call | solution.py:167
  31.2 0.0 copy-done.8
  31.2 0.0 copy-done.1
  31.2 0.0 copy-done.2
  31.2 32.4 %scores.1.partial = f32[16,2,16]{2,1,0:T(2,128)S(1)} custom-call(bf16[32,4,2048]{2,1,0:T(4,128)(2,1)S(1)} %bitcast.4, bf16[32,4,512]{2,1,0:T(4,128)(2,1)S(1)} %get-tuple-element.11.tg, bf16[16,4,2048]{2,1,0:T(4,128)(2,1)S(1)} %bitcast.5, bf16[16,4,512]{2,1,0:T(4,128)(2,1)S(1)} %get-tuple-element.13.qg, f32[32,8,128]{2,1,0:T(8,128)S(1)} %get-tuple-element.14.parts, ...), custom_call_target="tpu_custom_call" | custom-call | tf_op jit(solution)/shard_map/scores/pallas_call | solution.py:253
  63.6 0.0 copy-start.5
  63.6 0.6 copy-done.5
  64.2 9.3 %reduce_scores.1 = f32[2,16]{1,0:T(2,128)} custom-call(f32[16,2,16]{2,1,0:T(2,128)} %copy-done.5), custom_call_target="tpu_custom_call" | custom-call | tf_op jit(solution)/shard_map/reduce_scores/pallas_call | solution.py:300
  73.5 1.2 %copy.12 = f32[2,16]{1,0:T(2,128)} copy(f32[2,16]{1,0:T(2,128)} %reduce_scores.1) | data formatting | bytes 256
Async XLA Ops:
  0.0 31.2 %copy-start.8 = (s32[128]{0:T(128)S(1)}, s32[128]{0:T(128)}, u32[]{:S(2)}) copy-start(s32[128]{0:T(128)} %param.16) | copy-start | bytes 1540
  0.8 2.2 %copy-start = (f32[2048,512]{1,0:T(8,128)S(1)}, f32[2048,512]{1,0:T(8,128)}, u32[]{:S(2)}) copy-start(f32[2048,512]{1,0:T(8,128)} %eig.3) | copy-start | bytes 12582916
  2.9 0.8 %copy-start.3 = (bf16[4,8192]{1,0:T(4,128)(2,1)S(1)}, bf16[4,8192]{1,0:T(4,128)(2,1)}, u32[]{:S(2)}) copy-start(bf16[4,8192]{1,0:T(4,128)(2,1)} %tg.1) | copy-start | bytes 196612
  3.8 0.8 %copy-start.4 = (bf16[4,8192]{1,0:T(4,128)(2,1)S(1)}, bf16[4,8192]{1,0:T(4,128)(2,1)}, u32[]{:S(2)}) copy-start(bf16[4,8192]{1,0:T(4,128)(2,1)} %qg.1) | copy-start | bytes 196612
  4.6 0.8 %copy-start.6 = (bf16[4,4096]{1,0:T(4,128)(2,1)S(1)}, bf16[4,4096]{1,0:T(4,128)(2,1)}, u32[]{:S(2)}) copy-start(bf16[4,4096]{1,0:T(4,128)(2,1)} %ta.1) | copy-start | bytes 98308
  5.4 0.7 copy-start.7
  6.1 25.1 %copy-start.1 = (bf16[2048,512]{1,0:T(8,128)(2,1)S(1)}, bf16[2048,512]{1,0:T(8,128)(2,1)}, u32[]{:S(2)}) copy-start(bf16[2048,512]{1,0:T(8,128)(2,1)} %act_basis.1) | copy-start | bytes 6291460
  6.1 25.1 %copy-start.2 = (bf16[512,512]{1,0:T(8,128)(2,1)S(1)}, bf16[512,512]{1,0:T(8,128)(2,1)}, u32[]{:S(2)}) copy-start(bf16[512,512]{1,0:T(8,128)(2,1)} %grad_basis.1) | copy-start | bytes 1572868
  63.6 0.6 copy-start.5

commit v2 on v0

--- a/solution.py
+++ b/solution.py
@@ -1,12 +1,308 @@
+import functools
+
 import jax
 import jax.numpy as jnp
 from jax import lax
+from jax.experimental import pallas as pl
+from jax.experimental.pallas import tpu as pltpu
 from jax.sharding import PartitionSpec as P
 
 D = 4096
 FF = 8192
 QUERIES = 16
 EX_DP = 2
+PLANE = 4
+HALVES = 2
+MESH = pl.DeviceIdType.MESH
+
+
+def arrived(ref, sem):
+    pltpu.make_async_copy(ref, ref, sem).wait()
+
+
+def kernel(
+    groups, nblk,
+    ta, tg, qa, qg, act_basis, grad_basis, eig, qids, eids, out,
+    eig_v, ab_v, gb_v, ta_o, qa_o, tg_a, qg_a, tg_o, qg_o, part, parts_a, part_b, parts_b,
+    tf, gf, qf, qgf, act_t, grad_t, query_t, qmask, weight, score,
+    partial, slots_a, red, slots_b,
+    load_s, a_s, a_r, p_s, p_r, r_s, r_r,
+):
+    bf, f32 = jnp.bfloat16, jnp.float32
+    dp, blk = lax.axis_index("dp"), lax.axis_index("blk")
+    g, p = dp // PLANE, lax.rem(dp, PLANE)
+    gb = g * nblk + blk
+    column = groups * nblk
+    tok, qtok = ta.shape[0], qa.shape[0]
+    wa, wh, wg = qa.shape[1], ta_o.shape[-1], tg_o.shape[-1]
+    block = ab_v.shape[1]
+    across = lax.rem(p + 2, PLANE)
+    beside = p + 1 - 2 * lax.rem(p, 2)
+
+    loads = [pltpu.make_async_copy(src, dst, load_s.at[i]) for i, (src, dst) in enumerate(
+        ((eig, eig_v), (grad_basis, gb_v), (act_basis, ab_v)))]
+    for load in loads:
+        load.start()
+
+    in_column = []
+    for k in range(1, column):
+        to = lax.rem(gb + k, column)
+        in_column.append((to // nblk, lax.rem(to, nblk)))
+    in_row = [lax.rem(g + k, groups) for k in range(1, groups)]
+    in_plane = [lax.rem(p + k, PLANE) for k in range(1, PLANE)]
+
+    barrier = pltpu.get_barrier_semaphore()
+    for tg_, tb in in_column:
+        pl.semaphore_signal(barrier, inc=1, device_id=(tg_ * PLANE + p, tb), device_id_type=MESH)
+    for tp in in_plane:
+        pl.semaphore_signal(barrier, inc=1, device_id=(g * PLANE + tp, blk), device_id_type=MESH)
+    pl.semaphore_wait(barrier, column - 1 + PLANE - 1)
+
+    def remote(src, dst, send, recv, d, b):
+        return pltpu.make_async_remote_copy(
+            src, dst, send, recv, device_id=(d, b), device_id_type=MESH)
+
+    def columns(at, width):
+        return pl.ds(pl.multiple_of(at, 128), width)
+
+    def send_act(h):
+        for tg_ in in_row:
+            remote(qa.at[:, h * wh:(h + 1) * wh], qa_o.at[h, p, g], a_s.at[h], a_r.at[h],
+                   tg_ * PLANE + p, blk).start()
+        pltpu.make_async_copy(
+            qa.at[:, h * wh:(h + 1) * wh], qa_o.at[h, p, g], a_r.at[h]).start()
+        for tg_, tb in in_column:
+            remote(ta.at[:, columns(tb * wa + h * wh, wh)], ta_o.at[h, p, gb],
+                   a_s.at[2 + h], a_r.at[2 + h], tg_ * PLANE + p, tb).start()
+        pltpu.make_async_copy(
+            ta.at[:, columns(blk * wa + h * wh, wh)], ta_o.at[h, p, gb], a_r.at[2 + h]).start()
+
+    send_act(0)
+    wide = PLANE * wg
+    for tg_ in in_row:
+        remote(qg.at[:, columns(tg_ * wide, wide)], qg_a.at[g], a_s.at[4], a_r.at[4],
+               tg_ * PLANE + p, blk).start()
+    pltpu.make_async_copy(qg.at[:, columns(g * wide, wide)], qg_a.at[g], a_r.at[4]).start()
+    for tg_, tb in in_column:
+        remote(tg.at[:, columns(tg_ * wide, wide)], tg_a.at[gb], a_s.at[5], a_r.at[5],
+               tg_ * PLANE + p, tb).start()
+    pltpu.make_async_copy(tg.at[:, columns(g * wide, wide)], tg_a.at[gb], a_r.at[5]).start()
+
+    loads[0].wait()
+
+    def add(i, total):
+        rows = eig_v[pl.ds(pl.multiple_of(i * 128, 128), 128), :]
+        return total + jnp.sum(rows.reshape(16, 8, rows.shape[1]), axis=0)
+
+    total = lax.fori_loop(
+        0, eig_v.shape[0] // 128, add, jnp.zeros((8, eig_v.shape[1]), f32))
+    lanes = total[:, 0:128]
+    for c in range(1, eig_v.shape[1] // 128):
+        lanes = lanes + total[:, c * 128:(c + 1) * 128]
+    part[...] = lanes
+    for tg_, tb in in_column:
+        remote(part, parts_a.at[gb], a_s.at[6], a_r.at[6], tg_ * PLANE + p, tb).start()
+    pltpu.make_async_copy(part, parts_a.at[gb], a_r.at[6]).start()
+    send_act(1)
+
+    plane_sends = []
+
+    def to_plane(src, dst, at, tp):
+        copy = remote(src, dst, p_s.at[len(plane_sends)], p_r.at[at], g * PLANE + tp, blk)
+        copy.start()
+        plane_sends.append(copy)
+
+    def pass_on(h):
+        arrived(qa_o.at[h, p], a_r.at[h])
+        to_plane(qa_o.at[h, p], qa_o.at[h, p], 12 * h, across)
+        to_plane(qa_o.at[h, p], qa_o.at[h, p], 12 * h + 1, beside)
+        arrived(ta_o.at[h, p], a_r.at[2 + h])
+        to_plane(ta_o.at[h, p], ta_o.at[h, p], 12 * h + 2, across)
+        to_plane(ta_o.at[h, p], ta_o.at[h, p], 12 * h + 3, beside)
+
+    def pass_beside(h):
+        arrived(qa_o.at[h, p], p_r.at[12 * h])
+        to_plane(qa_o.at[h, across], qa_o.at[h, across], 12 * h + 4, beside)
+        arrived(ta_o.at[h, p], p_r.at[12 * h + 2])
+        to_plane(ta_o.at[h, across], ta_o.at[h, across], 12 * h + 5, beside)
+
+    def take(h):
+        arrived(qa_o.at[h, p], p_r.at[12 * h + 1])
+        arrived(qa_o.at[h, p], p_r.at[12 * h + 4])
+        arrived(ta_o.at[h, p], p_r.at[12 * h + 3])
+        arrived(ta_o.at[h, p], p_r.at[12 * h + 5])
+
+    def unpack(h):
+        for q in range(PLANE):
+            for e in range(groups):
+                row = (e * PLANE + q) * qtok
+                qf[row:row + qtok, :] = qa_o[h, q, e].astype(f32)
+                for b in range(nblk):
+                    row = ((e * PLANE + q) * nblk + b) * tok
+                    tf[row:row + tok, :] = ta_o[h, q, e * nblk + b].astype(f32)
+
+    pass_on(0)
+    arrived(qg_a, a_r.at[4])
+    for tp in in_plane:
+        to_plane(qg_a.at[:, :, columns(tp * wg, wg)], qg_o.at[p], 6, tp)
+    pltpu.make_async_copy(qg_a.at[:, :, columns(p * wg, wg)], qg_o.at[p], p_r.at[6]).start()
+    arrived(tg_a, a_r.at[5])
+    for tp in in_plane:
+        to_plane(tg_a.at[:, :, columns(tp * wg, wg)], tg_o.at[p], 7, tp)
+    pltpu.make_async_copy(tg_a.at[:, :, columns(p * wg, wg)], tg_o.at[p], p_r.at[7]).start()
+    arrived(parts_a, a_r.at[6])
+    part_b[...] = jnp.sum(parts_a[...], axis=0)
+    for tp in in_plane:
+        to_plane(part_b, parts_b.at[p], 8, tp)
+    pltpu.make_async_copy(part_b, parts_b.at[p], p_r.at[8]).start()
+    pass_beside(0)
+
+    loads[1].wait()
+    arrived(qg_o, p_r.at[6])
+    arrived(tg_o, p_r.at[7])
+    for q in range(PLANE):
+        for e in range(groups):
+            row = (e * PLANE + q) * qtok
+            qgf[row:row + qtok, :] = qg_o[q, e].astype(f32)
+            for b in range(nblk):
+                row = ((e * PLANE + q) * nblk + b) * tok
+                gf[row:row + tok, :] = tg_o[q, e * nblk + b].astype(f32)
+    turned = jnp.dot(gf[...].astype(bf), gb_v[...], preferred_element_type=f32)
+    grad_t[...] = turned.astype(bf).astype(f32).T.astype(bf)
+    qgrad = jnp.dot(
+        qgf[...].astype(bf), gb_v[...], preferred_element_type=f32).astype(bf).astype(f32)
+    qtokens = qids.shape[1]
+    one_query = (lax.broadcasted_iota(jnp.int32, (QUERIES, qtokens), 0) == qids[...]).astype(f32)
+    same = (lax.broadcasted_iota(jnp.int32, (qtokens, qtokens), 0)
+            == lax.broadcasted_iota(jnp.int32, (qtokens, qtokens), 1)).astype(f32)
+    of_token = lax.dot_general(
+        same.astype(bf), one_query.astype(bf), (((1,), (1,)), ((), ())),
+        preferred_element_type=f32)
+    for q in range(QUERIES):
+        qmask[q] = (qgrad * of_token[:, q:q + 1]).astype(bf)
+    score[...] = jnp.zeros_like(score)
+    loads[2].wait()
+    arrived(parts_b, p_r.at[8])
+    damping = 0.1 * jnp.sum(parts_b[...]) / (D * FF)
+    norm_scale = float(D * FF) ** (-0.5)
+    chunk = 256
+
+    def prepare(n):
+        at = slice(n * block, (n + 1) * block)
+        here = slice(n * block % wh, n * block % wh + block)
+        basis = ab_v[at, :]
+        turned = jnp.dot(tf[:, here].astype(bf), basis, preferred_element_type=f32)
+        act_t[...] = turned.astype(bf).astype(f32).T
+        turned = jnp.dot(qf[:, here].astype(bf), basis, preferred_element_type=f32)
+        query_t[...] = turned.astype(bf).astype(f32).T.astype(bf)
+        weight[...] = norm_scale / (eig_v[at, :] + damping)
+
+    def run(first, last):
+        @pl.loop(first, last, step=2)
+        def _(q0):
+            for q in (q0, q0 + 1):
+                total = score[q]
+                for c in range(0, block, chunk):
+                    rows = slice(c, c + chunk)
+                    gram = jnp.dot(query_t[rows, :], qmask[q], preferred_element_type=f32)
+                    precond = (gram * weight[rows, :]).astype(bf)
+                    mixed = jnp.dot(precond, grad_t[...], preferred_element_type=f32)
+                    mixed = mixed * act_t[rows, :]
+                    total = total + jnp.sum(
+                        mixed.reshape(chunk // 8, 8, mixed.shape[1]), axis=0)
+                score[q] = total
+
+    take(0)
+    unpack(0)
+    prepare(0)
+    run(0, QUERIES)
+    pass_on(1)
+    prepare(1)
+    run(0, QUERIES // 2)
+    pass_beside(1)
+    run(QUERIES // 2, QUERIES)
+    take(1)
+    unpack(1)
+    prepare(2)
+    run(0, QUERIES)
+    prepare(3)
+    run(0, QUERIES)
+
+    examples, tokens = partial.shape[0] * EX_DP, eids.shape[1]
+    one = (lax.broadcasted_iota(jnp.int32, (examples, tokens), 0) == eids[...]).astype(f32)
+    result = lax.dot_general(
+        one, jnp.sum(score[...], axis=1), (((1,), (1,)), ((), ())),
+        precision=lax.Precision.HIGHEST, preferred_element_type=f32)
+    for d in range(partial.shape[0]):
+        partial[d] = result[d * EX_DP:(d + 1) * EX_DP, :]
+    for tg_, tb in in_column:
+        remote(partial.at[pl.ds(tg_ * PLANE, PLANE)], slots_a.at[gb], r_s.at[0], r_r.at[0],
+               tg_ * PLANE + p, tb).start()
+    pltpu.make_async_copy(
+        partial.at[pl.ds(g * PLANE, PLANE)], slots_a.at[gb], r_r.at[0]).start()
+    for copy in plane_sends:
+        copy.wait_send()
+    for h in range(HALVES):
+        arrived(qa_o.at[h, p, 0:groups - 1], a_s.at[h])
+        arrived(ta_o.at[h, p, 0:column - 1], a_s.at[2 + h])
+    arrived(qg_a.at[0:groups - 1], a_s.at[4])
+    arrived(tg_a.at[0:column - 1], a_s.at[5])
+    arrived(parts_a.at[0:column - 1], a_s.at[6])
+    arrived(slots_a, r_r.at[0])
+    red[...] = jnp.sum(slots_a[...], axis=0)
+    for tp in in_plane:
+        remote(red.at[tp], slots_b.at[p], r_s.at[1], r_r.at[1], g * PLANE + tp, blk).start()
+    pltpu.make_async_copy(red.at[p], slots_b.at[p], r_r.at[1]).start()
+    arrived(slots_a.at[0:column - 1], r_s.at[0])
+    arrived(slots_b, r_r.at[1])
+    arrived(slots_b.at[0:PLANE - 1], r_s.at[1])
+    out[...] = jnp.sum(slots_b[...], axis=0)
+
+
+def shards_square(
+    ta, tg, qa, qg, act_basis, grad_basis, eig, example_ids, query_ids,
+):
+    ndp, nblk = lax.axis_size("dp"), lax.axis_size("blk")
+    groups = ndp // PLANE
+    column = groups * nblk
+    tok, qtok = ta.shape[0], qa.shape[0]
+    wa, wg = qa.shape[1], tg.shape[1] // ndp
+    wh = wa // HALVES
+    block = act_basis.shape[1]
+    tokens, qtokens = ndp * nblk * tok, ndp * qtok
+    bf, f32 = jnp.bfloat16, jnp.float32
+    dma = pltpu.SemaphoreType.DMA
+    vmem = pltpu.VMEM
+    full = pl.BlockSpec(memory_space=pltpu.VMEM)
+    far = pl.BlockSpec(memory_space=pl.ANY)
+    return pl.pallas_call(
+        functools.partial(kernel, groups, nblk),
+        out_shape=jax.ShapeDtypeStruct((EX_DP, QUERIES), f32),
+        in_specs=[far] * 7 + [full] * 2,
+        out_specs=full,
+        scratch_shapes=[
+            vmem(eig.shape, f32), vmem(act_basis.shape, bf), vmem(grad_basis.shape, bf),
+            vmem((HALVES, PLANE, column, tok, wh), bf),
+            vmem((HALVES, PLANE, groups, qtok, wh), bf),
+            vmem((column, tok, PLANE * wg), bf), vmem((groups, qtok, PLANE * wg), bf),
+            vmem((PLANE, column, tok, wg), bf), vmem((PLANE, groups, qtok, wg), bf),
+            vmem((8, 128), f32), vmem((column, 8, 128), f32),
+            vmem((8, 128), f32), vmem((PLANE, 8, 128), f32),
+            vmem((tokens, wh), f32), vmem((tokens, wg), f32),
+            vmem((qtokens, wh), f32), vmem((qtokens, wg), f32),
+            vmem((block, tokens), f32), vmem((wg, tokens), bf),
+            vmem((block, qtokens), bf), vmem((QUERIES, qtokens, wg), bf),
+            vmem((block, wg), f32), vmem((QUERIES, 8, tokens), f32),
+            vmem((ndp, EX_DP, QUERIES), f32), vmem((column, PLANE, EX_DP, QUERIES), f32),
+            vmem((PLANE, EX_DP, QUERIES), f32), vmem((PLANE, EX_DP, QUERIES), f32),
+            dma((3,)), dma((7,)), dma((7,)), dma((32,)), dma((20,)),
+            dma((2,)), dma((2,)),
+        ],
+        compiler_params=pltpu.CompilerParams(
+            collective_id=0, has_side_effects=True, vmem_limit_bytes=56 * 2**20
+        ),
+        name="influence",
+    )(ta, tg, qa, qg, act_basis, grad_basis, eig, query_ids[None, :], example_ids[None, :])
 
 
 def as_sent(x):
@@ -140,6 +436,18 @@
         P(),
         P(),
     )
-    return jax.shard_map(
-        shards, mesh=mesh, in_specs=placed, out_specs=P("dp", None), check_vma=False
-    )
+    ndp = mesh.shape["dp"]
+
+    def run(*arrays):
+        block = arrays[4].shape[1]
+        square = (
+            arrays[5].shape[1] == block * ndp
+            and arrays[4].shape[0] == 4 * block * mesh.shape["blk"]
+            and ndp % PLANE == 0
+        )
+        return jax.shard_map(
+            shards_square if square else shards,
+            mesh=mesh, in_specs=placed, out_specs=P("dp", None), check_vma=False
+        )(*arrays)
+
+    return run

time: 185 us -> 64 us (0.35)
  blocking collectives: 130 us -> 0 us
  Pallas kernels: 0 us -> 62.6 us
  matrix products: 23.9 us -> 0 us
  starting transfers between devices: 11.9 us -> 0 us
  other arithmetic: 8.68 us -> 0 us
  local copies, waits for them, and re-layouts: 7.72 us -> 1.24 us
    psum x2 -> x0, blocking collectives: 79.9 us -> none  [the longest x1 41.7 us: shards(): eigen_sum = lax.psum(jnp.sum(eigenvalues), ('dp', 'blk'))]
    pallas_call x0 -> x1, Pallas kernels: none -> 62.6 us  [shards_square(): pl.pallas_call(functools.partial(kernel, groups, nblk), out_shape=jax.Sha...]
    all_gather x3 -> x0, blocking collectives: 49.9 us -> none  [the longest x1 23.2 us: shards(): lax.all_gather(rotate_blocks(owned_rows, act_basis), 'dp', axis=0, tiled=...]
    dot_general x6 -> x0, matrix products: 23.9 us -> none  [the longest x1 22.5 us: shards(): jnp.dot(shard_rows, precond, preferred_element_type=jnp.float32)]
    all_to_all x3 -> x0, starting transfers between devices: 11.9 us -> none  [the longest x1 4.23 us: shards(): lax.all_to_all(train_act, 'blk', split_axis=1, concat_axis=0, tiled=True)]
    add x1 -> x0, local copies, waits for them, and re-layouts: 5.43 us -> none  [shards(): eigenvalues[:, None, :] + damping]
    add x1 -> x0, other arithmetic: 4.66 us -> none  [shards(): eigenvalues[:, None, :] + damping]
    reduce_sum x1 -> x0, other arithmetic: 4.02 us -> none  [shards(): eigen_sum = lax.psum(jnp.sum(eigenvalues), ('dp', 'blk'))]
  transfers between devices with their start and end apart: 3 -> 0, of which waited for: 1 -> 0; matrix products, arithmetic and copies ran while one was open for 6% -> 0% of each run, Pallas kernels for 0% -> 0%
where the time goes in v2:
time: 64 us; the launch traced here: 63.9 us
  Pallas kernels  62.6 us (98%)
  local copies, waits for them, and re-layouts  1.24 us (2%)
    pallas_call x1, Pallas kernels, shards_square(): pl.pallas_call(functools.partial(kernel, groups, nblk), out_shape=jax.Sha...  62.6 us

profile of v2, /device:TPU:0, one launch (start us, length us, event | category | flops | bytes accessed | tf_op | source)
XLA Modules:
  0.0 63.9 jit_solution(12367609491283771110)
XLA Ops:
  0.0 62.6 %influence.1 = f32[2,16]{1,0:T(2,128)} custom-call(bf16[4,4096]{1,0:T(4,128)(2,1)} %ta.1, bf16[4,8192]{1,0:T(4,128)(2,1)} %tg.1, bf16[4,2048]{1,0:T(4,128)(2,1)} %qa.1, bf16[4,8192]{1,0:T(4,128)(2,1)} %qg.1, bf16[2048,512]{1,0:T(8,128)(2,1)} %act_basis.1, bf16[512,512]{1,0:T(8,128)(2,1)} %grad_basis.1, f32[2048,512]{1,0:T(8,128)} %eig.1, s32[1,64]{1,0:T(1,128)} %bitcast.2, ...), custom_call_target="tpu_custom_call" | custom-call | tf_op jit(solution)/shard_map/influence/pallas_call | solution.py:278
  62.6 1.2 %copy.11 = f32[2,16]{1,0:T(2,128)} copy(f32[2,16]{1,0:T(2,128)} %influence.1) | data formatting | bytes 256

commit v3 on v2

--- a/solution.py
+++ b/solution.py
@@ -24,7 +24,7 @@
     groups, nblk,
     ta, tg, qa, qg, act_basis, grad_basis, eig, qids, eids, out,
     eig_v, ab_v, gb_v, ta_o, qa_o, tg_a, qg_a, tg_o, qg_o, part, parts_a, part_b, parts_b,
-    tf, gf, qf, qgf, act_t, grad_t, query_t, qmask, weight, score,
+    tf, gf, qf, qgf, act, grad, query_t, qmask, weight, even, odd, score,
     partial, slots_a, red, slots_b,
     load_s, a_s, a_r, p_s, p_r, r_s, r_r,
 ):
@@ -168,7 +168,7 @@
                 row = ((e * PLANE + q) * nblk + b) * tok
                 gf[row:row + tok, :] = tg_o[q, e * nblk + b].astype(f32)
     turned = jnp.dot(gf[...].astype(bf), gb_v[...], preferred_element_type=f32)
-    grad_t[...] = turned.astype(bf).astype(f32).T.astype(bf)
+    grad[...] = turned.astype(bf).astype(f32)
     qgrad = jnp.dot(
         qgf[...].astype(bf), gb_v[...], preferred_element_type=f32).astype(bf).astype(f32)
     qtokens = qids.shape[1]
@@ -192,46 +192,65 @@
         here = slice(n * block % wh, n * block % wh + block)
         basis = ab_v[at, :]
         turned = jnp.dot(tf[:, here].astype(bf), basis, preferred_element_type=f32)
-        act_t[...] = turned.astype(bf).astype(f32).T
+        act[...] = turned.astype(bf)
         turned = jnp.dot(qf[:, here].astype(bf), basis, preferred_element_type=f32)
         query_t[...] = turned.astype(bf).astype(f32).T.astype(bf)
         weight[...] = norm_scale / (eig_v[at, :] + damping)
 
-    def run(first, last):
-        @pl.loop(first, last, step=2)
-        def _(q0):
-            for q in (q0, q0 + 1):
-                total = score[q]
-                for c in range(0, block, chunk):
-                    rows = slice(c, c + chunk)
-                    gram = jnp.dot(query_t[rows, :], qmask[q], preferred_element_type=f32)
-                    precond = (gram * weight[rows, :]).astype(bf)
-                    mixed = jnp.dot(precond, grad_t[...], preferred_element_type=f32)
-                    mixed = mixed * act_t[rows, :]
-                    total = total + jnp.sum(
-                        mixed.reshape(chunk // 8, 8, mixed.shape[1]), axis=0)
-                score[q] = total
+    def precondition(q, slot, rows):
+        for c in range(0, wg, chunk):
+            cols = slice(c, c + chunk)
+            gram = jnp.dot(query_t[rows, :], qmask[q, :, cols], preferred_element_type=f32)
+            slot[rows, cols] = (gram * weight[rows, cols]).astype(bf)
+
+    def step(q, now, later):
+        mixed = None
+        for c in range(0, block, chunk):
+            rows = slice(c, c + chunk)
+            term = jnp.dot(act[:, rows], now[rows, :], preferred_element_type=f32)
+            if later is not None:
+                precondition(q + 1, later, rows)
+            mixed = term if mixed is None else mixed + term
+        mixed = mixed * grad[...]
+        total = mixed[:, 0:128]
+        for c in range(128, wg, 128):
+            total = total + mixed[:, c:c + 128]
+        score[q] = score[q] + total
+
+    def run(first, last, starts, ends):
+        if starts:
+            for c in range(0, block, chunk):
+                precondition(0, even, slice(c, c + chunk))
+
+        @pl.loop(first, last - 2 if ends else last, step=2)
+        def _(q):
+            step(q, even, odd)
+            step(q + 1, odd, even)
+
+        if ends:
+            step(last - 2, even, odd)
+            step(last - 1, odd, None)
 
     take(0)
     unpack(0)
     prepare(0)
-    run(0, QUERIES)
+    run(0, QUERIES, True, True)
     pass_on(1)
     prepare(1)
-    run(0, QUERIES // 2)
+    run(0, QUERIES // 2, True, False)
     pass_beside(1)
-    run(QUERIES // 2, QUERIES)
+    run(QUERIES // 2, QUERIES, False, True)
     take(1)
     unpack(1)
     prepare(2)
-    run(0, QUERIES)
+    run(0, QUERIES, True, True)
     prepare(3)
-    run(0, QUERIES)
+    run(0, QUERIES, True, True)
 
     examples, tokens = partial.shape[0] * EX_DP, eids.shape[1]
     one = (lax.broadcasted_iota(jnp.int32, (examples, tokens), 0) == eids[...]).astype(f32)
     result = lax.dot_general(
-        one, jnp.sum(score[...], axis=1), (((1,), (1,)), ((), ())),
+        one, jnp.sum(score[...], axis=2), (((1,), (1,)), ((), ())),
         precision=lax.Precision.HIGHEST, preferred_element_type=f32)
     for d in range(partial.shape[0]):
         partial[d] = result[d * EX_DP:(d + 1) * EX_DP, :]
@@ -290,9 +309,10 @@
             vmem((8, 128), f32), vmem((PLANE, 8, 128), f32),
             vmem((tokens, wh), f32), vmem((tokens, wg), f32),
             vmem((qtokens, wh), f32), vmem((qtokens, wg), f32),
-            vmem((block, tokens), f32), vmem((wg, tokens), bf),
+            vmem((tokens, block), bf), vmem((tokens, wg), f32),
             vmem((block, qtokens), bf), vmem((QUERIES, qtokens, wg), bf),
-            vmem((block, wg), f32), vmem((QUERIES, 8, tokens), f32),
+            vmem((block, wg), f32), vmem((block, wg), bf), vmem((block, wg), bf),
+            vmem((QUERIES, tokens, 128), f32),
             vmem((ndp, EX_DP, QUERIES), f32), vmem((column, PLANE, EX_DP, QUERIES), f32),
             vmem((PLANE, EX_DP, QUERIES), f32), vmem((PLANE, EX_DP, QUERIES), f32),
             dma((3,)), dma((7,)), dma((7,)), dma((32,)), dma((20,)),

time: 64 us -> 53 us (0.83)
  Pallas kernels: 62.6 us -> 51.6 us
    pallas_call x1, Pallas kernels: 62.6 us -> 51.6 us  [shards_square(): pl.pallas_call(functools.partial(kernel, groups, nblk), out_shape=jax.Sha...]
where the time goes in v3:
time: 53 us; the launch traced here: 52.9 us
  Pallas kernels  51.6 us (97%)
  local copies, waits for them, and re-layouts  1.24 us (2%)
    pallas_call x1, Pallas kernels, shards_square(): pl.pallas_call(functools.partial(kernel, groups, nblk), out_shape=jax.Sha...  51.6 us
    unnamed x1, local copies, waits for them, and re-layouts  1.24 us

profile of v3, /device:TPU:0, one launch (start us, length us, event | category | flops | bytes accessed | tf_op | source)
XLA Modules:
  0.0 52.9 jit_solution(11508217125792050890)
XLA Ops:
  0.0 51.6 %influence.1 = f32[2,16]{1,0:T(2,128)} custom-call(bf16[4,4096]{1,0:T(4,128)(2,1)} %ta.1, bf16[4,8192]{1,0:T(4,128)(2,1)} %tg.1, bf16[4,2048]{1,0:T(4,128)(2,1)} %qa.1, bf16[4,8192]{1,0:T(4,128)(2,1)} %qg.1, bf16[2048,512]{1,0:T(8,128)(2,1)} %act_basis.1, bf16[512,512]{1,0:T(8,128)(2,1)} %grad_basis.1, f32[2048,512]{1,0:T(8,128)} %eig.1, s32[1,64]{1,0:T(1,128)} %bitcast.2, ...), custom_call_target="tpu_custom_call" | custom-call | tf_op jit(solution)/shard_map/influence/pallas_call | solution.py:297
  51.6 1.2 %copy.11 = f32[2,16]{1,0:T(2,128)} copy(f32[2,16]{1,0:T(2,128)} %influence.1) | data formatting | bytes 256

commit v4 on v3

--- a/solution.py
+++ b/solution.py
@@ -24,7 +24,7 @@
     groups, nblk,
     ta, tg, qa, qg, act_basis, grad_basis, eig, qids, eids, out,
     eig_v, ab_v, gb_v, ta_o, qa_o, tg_a, qg_a, tg_o, qg_o, part, parts_a, part_b, parts_b,
-    tf, gf, qf, qgf, act, grad, query_t, qmask, weight, even, odd, score,
+    tf, gf, qf, qgf, act, grad, query_t, qmask, weight, even, odd, score, by_query,
     partial, slots_a, red, slots_b,
     load_s, a_s, a_r, p_s, p_r, r_s, r_r,
 ):
@@ -103,28 +103,36 @@
     for tg_, tb in in_column:
         remote(part, parts_a.at[gb], a_s.at[6], a_r.at[6], tg_ * PLANE + p, tb).start()
     pltpu.make_async_copy(part, parts_a.at[gb], a_r.at[6]).start()
-    send_act(1)
 
     plane_sends = []
 
     def to_plane(src, dst, at, tp):
         copy = remote(src, dst, p_s.at[len(plane_sends)], p_r.at[at], g * PLANE + tp, blk)
-        copy.start()
         plane_sends.append(copy)
+        return copy
+
+    early, late = [], []
+    for h in range(HALVES):
+        early.append([
+            to_plane(buf.at[h, p], buf.at[h, p], 12 * h + 2 * i + k, tp)
+            for i, buf in enumerate((qa_o, ta_o)) for k, tp in enumerate((across, beside))])
+        late.append([
+            to_plane(buf.at[h, across], buf.at[h, across], 12 * h + 4 + i, beside)
+            for i, buf in enumerate((qa_o, ta_o))])
 
     def pass_on(h):
         arrived(qa_o.at[h, p], a_r.at[h])
-        to_plane(qa_o.at[h, p], qa_o.at[h, p], 12 * h, across)
-        to_plane(qa_o.at[h, p], qa_o.at[h, p], 12 * h + 1, beside)
+        early[h][0].start()
+        early[h][1].start()
         arrived(ta_o.at[h, p], a_r.at[2 + h])
-        to_plane(ta_o.at[h, p], ta_o.at[h, p], 12 * h + 2, across)
-        to_plane(ta_o.at[h, p], ta_o.at[h, p], 12 * h + 3, beside)
+        early[h][2].start()
+        early[h][3].start()
 
     def pass_beside(h):
         arrived(qa_o.at[h, p], p_r.at[12 * h])
-        to_plane(qa_o.at[h, across], qa_o.at[h, across], 12 * h + 4, beside)
+        late[h][0].start()
         arrived(ta_o.at[h, p], p_r.at[12 * h + 2])
-        to_plane(ta_o.at[h, across], ta_o.at[h, across], 12 * h + 5, beside)
+        late[h][1].start()
 
     def take(h):
         arrived(qa_o.at[h, p], p_r.at[12 * h + 1])
@@ -144,16 +152,17 @@
     pass_on(0)
     arrived(qg_a, a_r.at[4])
     for tp in in_plane:
-        to_plane(qg_a.at[:, :, columns(tp * wg, wg)], qg_o.at[p], 6, tp)
+        to_plane(qg_a.at[:, :, columns(tp * wg, wg)], qg_o.at[p], 6, tp).start()
     pltpu.make_async_copy(qg_a.at[:, :, columns(p * wg, wg)], qg_o.at[p], p_r.at[6]).start()
     arrived(tg_a, a_r.at[5])
     for tp in in_plane:
-        to_plane(tg_a.at[:, :, columns(tp * wg, wg)], tg_o.at[p], 7, tp)
+        to_plane(tg_a.at[:, :, columns(tp * wg, wg)], tg_o.at[p], 7, tp).start()
     pltpu.make_async_copy(tg_a.at[:, :, columns(p * wg, wg)], tg_o.at[p], p_r.at[7]).start()
+    send_act(1)
     arrived(parts_a, a_r.at[6])
     part_b[...] = jnp.sum(parts_a[...], axis=0)
     for tp in in_plane:
-        to_plane(part_b, parts_b.at[p], 8, tp)
+        to_plane(part_b, parts_b.at[p], 8, tp).start()
     pltpu.make_async_copy(part_b, parts_b.at[p], p_r.at[8]).start()
     pass_beside(0)
 
@@ -187,73 +196,100 @@
     norm_scale = float(D * FF) ** (-0.5)
     chunk = 256
 
+    count_blocks = wa // block
+    in_half = wh // block
+
     def prepare(n):
-        at = slice(n * block, (n + 1) * block)
-        here = slice(n * block % wh, n * block % wh + block)
+        slot = lax.rem(n, 2)
+        at = pl.ds(pl.multiple_of(n * block, block), block)
+        here = pl.ds(pl.multiple_of(lax.rem(n, in_half) * block, block), block)
         basis = ab_v[at, :]
         turned = jnp.dot(tf[:, here].astype(bf), basis, preferred_element_type=f32)
-        act[...] = turned.astype(bf)
+        act[slot] = turned.astype(bf)
         turned = jnp.dot(qf[:, here].astype(bf), basis, preferred_element_type=f32)
-        query_t[...] = turned.astype(bf).astype(f32).T.astype(bf)
-        weight[...] = norm_scale / (eig_v[at, :] + damping)
-
-    def precondition(q, slot, rows):
+        query_t[slot] = turned.astype(bf).astype(f32).T.astype(bf)
+        weight[slot] = norm_scale / (eig_v[at, :] + damping)
+
+    def precondition(at, q, held, rows):
         for c in range(0, wg, chunk):
             cols = slice(c, c + chunk)
-            gram = jnp.dot(query_t[rows, :], qmask[q, :, cols], preferred_element_type=f32)
-            slot[rows, cols] = (gram * weight[rows, cols]).astype(bf)
-
-    def step(q, now, later):
+            gram = jnp.dot(query_t[at, rows, :], qmask[q, :, cols], preferred_element_type=f32)
+            held[rows, cols] = (gram * weight[at, rows, cols]).astype(bf)
+
+    def step(at, q, now, later, next_at, next_q, last):
         mixed = None
         for c in range(0, block, chunk):
             rows = slice(c, c + chunk)
-            term = jnp.dot(act[:, rows], now[rows, :], preferred_element_type=f32)
+            term = jnp.dot(act[at, :, rows], now[rows, :], preferred_element_type=f32)
             if later is not None:
-                precondition(q + 1, later, rows)
+                precondition(next_at, next_q, later, rows)
             mixed = term if mixed is None else mixed + term
         mixed = mixed * grad[...]
-        total = mixed[:, 0:128]
-        for c in range(128, wg, 128):
+        total = score[q]
+        for c in range(0, wg, 128):
             total = total + mixed[:, c:c + 128]
-        score[q] = score[q] + total
-
-    def run(first, last, starts, ends):
-        if starts:
-            for c in range(0, block, chunk):
-                precondition(0, even, slice(c, c + chunk))
-
-        @pl.loop(first, last - 2 if ends else last, step=2)
+        if last:
+            lane = lax.broadcasted_iota(jnp.int32, total.shape, 1)
+            by_query[...] = jnp.where(
+                lane == q, jnp.sum(total, axis=1, keepdims=True), by_query[...])
+        else:
+            score[q] = total
+
+    def run(at, first, last, final):
+        @pl.loop(first, last, step=4)
         def _(q):
-            step(q, even, odd)
-            step(q + 1, odd, even)
-
-        if ends:
-            step(last - 2, even, odd)
-            step(last - 1, odd, None)
+            step(at, q, even, odd, at, q + 1, final)
+            step(at, q + 1, odd, even, at, q + 2, final)
+            step(at, q + 2, even, odd, at, q + 3, final)
+            step(at, q + 3, odd, even, at, q + 4, final)
+
+    def tail(at, final):
+        q = QUERIES - 4
+        step(at, q, even, odd, at, q + 1, final)
+        step(at, q + 1, odd, even, at, q + 2, final)
+        step(at, q + 2, even, odd, at, q + 3, final)
+        step(at, q + 3, odd, None if final else even, 1 - at, 0, final)
 
     take(0)
     unpack(0)
+    by_query[...] = jnp.zeros_like(by_query)
     prepare(0)
-    run(0, QUERIES, True, True)
-    pass_on(1)
-    prepare(1)
-    run(0, QUERIES // 2, True, False)
-    pass_beside(1)
-    run(QUERIES // 2, QUERIES, False, True)
-    take(1)
-    unpack(1)
-    prepare(2)
-    run(0, QUERIES, True, True)
-    prepare(3)
-    run(0, QUERIES, True, True)
+    for c in range(0, block, chunk):
+        precondition(0, 0, even, slice(c, c + chunk))
+
+    @pl.loop(0, count_blocks - 1)
+    def _(n):
+        at = lax.rem(n, 2)
+        run(at, 0, QUERIES - 8, False)
+
+        @pl.when(n == 0)
+        def _():
+            pass_on(1)
+
+        @pl.when(n == 1)
+        def _():
+            pass_beside(1)
+
+        run(at, QUERIES - 8, QUERIES - 4, False)
+
+        @pl.when(n == in_half - 1)
+        def _():
+            take(1)
+            unpack(1)
+
+        prepare(n + 1)
+        tail(at, False)
+
+    run((count_blocks - 1) % 2, 0, QUERIES - 4, True)
+    tail((count_blocks - 1) % 2, True)
 
     examples, tokens = partial.shape[0] * EX_DP, eids.shape[1]
     one = (lax.broadcasted_iota(jnp.int32, (examples, tokens), 0) == eids[...]).astype(f32)
     result = lax.dot_general(
-        one, jnp.sum(score[...], axis=2), (((1,), (1,)), ((), ())),
+        one, by_query[...], (((1,), (0,)), ((), ())),
         precision=lax.Precision.HIGHEST, preferred_element_type=f32)
     for d in range(partial.shape[0]):
-        partial[d] = result[d * EX_DP:(d + 1) * EX_DP, :]
+        partial[d] = result[d * EX_DP:(d + 1) * EX_DP, 0:QUERIES]
     for tg_, tb in in_column:
         remote(partial.at[pl.ds(tg_ * PLANE, PLANE)], slots_a.at[gb], r_s.at[0], r_r.at[0],
                tg_ * PLANE + p, tb).start()
@@ -309,10 +345,10 @@
             vmem((8, 128), f32), vmem((PLANE, 8, 128), f32),
             vmem((tokens, wh), f32), vmem((tokens, wg), f32),
             vmem((qtokens, wh), f32), vmem((qtokens, wg), f32),
-            vmem((tokens, block), bf), vmem((tokens, wg), f32),
-            vmem((block, qtokens), bf), vmem((QUERIES, qtokens, wg), bf),
-            vmem((block, wg), f32), vmem((block, wg), bf), vmem((block, wg), bf),
-            vmem((QUERIES, tokens, 128), f32),
+            vmem((2, tokens, block), bf), vmem((tokens, wg), f32),
+            vmem((2, block, qtokens), bf), vmem((QUERIES, qtokens, wg), bf),
+            vmem((2, block, wg), f32), vmem((block, wg), bf), vmem((block, wg), bf),
+            vmem((QUERIES, tokens, 128), f32), vmem((tokens, 128), f32),
             vmem((ndp, EX_DP, QUERIES), f32), vmem((column, PLANE, EX_DP, QUERIES), f32),
             vmem((PLANE, EX_DP, QUERIES), f32), vmem((PLANE, EX_DP, QUERIES), f32),
             dma((3,)), dma((7,)), dma((7,)), dma((32,)), dma((20,)),

time: 53 us -> 48.4 us (0.913)
  Pallas kernels: 51.6 us -> 47 us
    pallas_call x1, Pallas kernels: 51.6 us -> 47 us  [shards_square(): pl.pallas_call(functools.partial(kernel, groups, nblk), out_shape=jax.Sha...]
where the time goes in v4:
time: 48.4 us; the launch traced here: 48.2 us
  Pallas kernels  47 us (97%)
  local copies, waits for them, and re-layouts  1.24 us (3%)
    pallas_call x1, Pallas kernels, shards_square(): pl.pallas_call(functools.partial(kernel, groups, nblk), out_shape=jax.Sha...  47 us
    unnamed x1, local copies, waits for them, and re-layouts  1.24 us

profile of v4, /device:TPU:0, one launch (start us, length us, event | category | flops | bytes accessed | tf_op | source)
XLA Modules:
  0.0 48.2 jit_solution(8854118304443083380)
XLA Ops:
  0.0 47.0 %influence.1 = f32[2,16]{1,0:T(2,128)} custom-call(bf16[4,4096]{1,0:T(4,128)(2,1)} %ta.1, bf16[4,8192]{1,0:T(4,128)(2,1)} %tg.1, bf16[4,2048]{1,0:T(4,128)(2,1)} %qa.1, bf16[4,8192]{1,0:T(4,128)(2,1)} %qg.1, bf16[2048,512]{1,0:T(8,128)(2,1)} %act_basis.1, bf16[512,512]{1,0:T(8,128)(2,1)} %grad_basis.1, f32[2048,512]{1,0:T(8,128)} %eig.1, s32[1,64]{1,0:T(1,128)} %bitcast.2, ...), custom_call_target="tpu_custom_call" | custom-call | tf_op jit(solution)/shard_map/influence/pallas_call | solution.py:333
  47.0 1.2 %copy.11 = f32[2,16]{1,0:T(2,128)} copy(f32[2,16]{1,0:T(2,128)} %influence.1) | data formatting | bytes 256

commit v5 on v4

--- a/solution.py
+++ b/solution.py
@@ -210,24 +210,21 @@
         query_t[slot] = turned.astype(bf).astype(f32).T.astype(bf)
         weight[slot] = norm_scale / (eig_v[at, :] + damping)
 
-    def precondition(at, q, held, rows):
+    def precondition(at, q, held, cols):
+        for r in range(0, block, chunk):
+            rows = slice(r, r + chunk)
+            gram = jnp.dot(query_t[at, rows, :], qmask[q, :, cols], preferred_element_type=f32)
+            held[rows, cols] = (gram * weight[at, rows, cols]).astype(bf)
+
+    def step(at, q, now, later, next_at, next_q, last):
+        total = score[q]
         for c in range(0, wg, chunk):
             cols = slice(c, c + chunk)
-            gram = jnp.dot(query_t[at, rows, :], qmask[q, :, cols], preferred_element_type=f32)
-            held[rows, cols] = (gram * weight[at, rows, cols]).astype(bf)
-
-    def step(at, q, now, later, next_at, next_q, last):
-        mixed = None
-        for c in range(0, block, chunk):
-            rows = slice(c, c + chunk)
-            term = jnp.dot(act[at, :, rows], now[rows, :], preferred_element_type=f32)
+            mixed = jnp.dot(act[at], now[:, cols], preferred_element_type=f32) * grad[:, cols]
+            for k in range(0, chunk, 128):
+                total = total + mixed[:, k:k + 128]
             if later is not None:
-                precondition(next_at, next_q, later, rows)
-            mixed = term if mixed is None else mixed + term
-        mixed = mixed * grad[...]
-        total = score[q]
-        for c in range(0, wg, 128):
-            total = total + mixed[:, c:c + 128]
+                precondition(next_at, next_q, later, cols)
         if last:
             lane = lax.broadcasted_iota(jnp.int32, total.shape, 1)
             by_query[...] = jnp.where(
@@ -254,7 +251,7 @@
     unpack(0)
     by_query[...] = jnp.zeros_like(by_query)
     prepare(0)
-    for c in range(0, block, chunk):
+    for c in range(0, wg, chunk):
         precondition(0, 0, even, slice(c, c + chunk))
 
     @pl.loop(0, count_blocks - 1)

time: 48.4 us -> 48.6 us (level)
  no operation moved by 1% of the time
where the time goes in v5:
time: 48.6 us; the launch traced here: 48.5 us
  Pallas kernels  47.2 us (97%)
  local copies, waits for them, and re-layouts  1.24 us (3%)
    pallas_call x1, Pallas kernels, shards_square(): pl.pallas_call(functools.partial(kernel, groups, nblk), out_shape=jax.Sha...  47.2 us
    unnamed x1, local copies, waits for them, and re-layouts  1.24 us

profile of v5, /device:TPU:0, one launch (start us, length us, event | category | flops | bytes accessed | tf_op | source)
XLA Modules:
  0.0 48.5 jit_solution(10628369040681060370)
XLA Ops:
  0.0 47.2 %influence.1 = f32[2,16]{1,0:T(2,128)} custom-call(bf16[4,4096]{1,0:T(4,128)(2,1)} %ta.1, bf16[4,8192]{1,0:T(4,128)(2,1)} %tg.1, bf16[4,2048]{1,0:T(4,128)(2,1)} %qa.1, bf16[4,8192]{1,0:T(4,128)(2,1)} %qg.1, bf16[2048,512]{1,0:T(8,128)(2,1)} %act_basis.1, bf16[512,512]{1,0:T(8,128)(2,1)} %grad_basis.1, f32[2048,512]{1,0:T(8,128)} %eig.1, s32[1,64]{1,0:T(1,128)} %bitcast.2, ...), custom_call_target="tpu_custom_call" | custom-call | tf_op jit(solution)/shard_map/influence/pallas_call | solution.py:330
  47.2 1.2 %copy.11 = f32[2,16]{1,0:T(2,128)} copy(f32[2,16]{1,0:T(2,128)} %influence.1) | data formatting | bytes 256

commit v6 on v4

--- a/solution.py
+++ b/solution.py
@@ -51,12 +51,17 @@
     in_row = [lax.rem(g + k, groups) for k in range(1, groups)]
     in_plane = [lax.rem(p + k, PLANE) for k in range(1, PLANE)]
 
+    other_blk = [lax.rem(blk + k, nblk) for k in range(1, nblk)]
+
     barrier = pltpu.get_barrier_semaphore()
     for tg_, tb in in_column:
         pl.semaphore_signal(barrier, inc=1, device_id=(tg_ * PLANE + p, tb), device_id_type=MESH)
     for tp in in_plane:
         pl.semaphore_signal(barrier, inc=1, device_id=(g * PLANE + tp, blk), device_id_type=MESH)
-    pl.semaphore_wait(barrier, column - 1 + PLANE - 1)
+        for tb in other_blk:
+            pl.semaphore_signal(
+                barrier, inc=1, device_id=(g * PLANE + tp, tb), device_id_type=MESH)
+    pl.semaphore_wait(barrier, column - 1 + (PLANE - 1) * nblk)
 
     def remote(src, dst, send, recv, d, b):
         return pltpu.make_async_remote_copy(
@@ -83,10 +88,10 @@
         remote(qg.at[:, columns(tg_ * wide, wide)], qg_a.at[g], a_s.at[4], a_r.at[4],
                tg_ * PLANE + p, blk).start()
     pltpu.make_async_copy(qg.at[:, columns(g * wide, wide)], qg_a.at[g], a_r.at[4]).start()
-    for tg_, tb in in_column:
-        remote(tg.at[:, columns(tg_ * wide, wide)], tg_a.at[gb], a_s.at[5], a_r.at[5],
-               tg_ * PLANE + p, tb).start()
-    pltpu.make_async_copy(tg.at[:, columns(g * wide, wide)], tg_a.at[gb], a_r.at[5]).start()
+    for tg_ in in_row:
+        remote(tg.at[:, columns(tg_ * wide, wide)], tg_a.at[g], a_s.at[5], a_r.at[5],
+               tg_ * PLANE + p, blk).start()
+    pltpu.make_async_copy(tg.at[:, columns(g * wide, wide)], tg_a.at[g], a_r.at[5]).start()
 
     loads[0].wait()
 
@@ -106,8 +111,8 @@
 
     plane_sends = []
 
-    def to_plane(src, dst, at, tp):
-        copy = remote(src, dst, p_s.at[len(plane_sends)], p_r.at[at], g * PLANE + tp, blk)
+    def to_plane(src, dst, at, tp, b=blk):
+        copy = remote(src, dst, p_s.at[len(plane_sends)], p_r.at[at], g * PLANE + tp, b)
         plane_sends.append(copy)
         return copy
 
@@ -156,8 +161,12 @@
     pltpu.make_async_copy(qg_a.at[:, :, columns(p * wg, wg)], qg_o.at[p], p_r.at[6]).start()
     arrived(tg_a, a_r.at[5])
     for tp in in_plane:
-        to_plane(tg_a.at[:, :, columns(tp * wg, wg)], tg_o.at[p], 7, tp).start()
-    pltpu.make_async_copy(tg_a.at[:, :, columns(p * wg, wg)], tg_o.at[p], p_r.at[7]).start()
+        to_plane(tg_a.at[:, :, columns(tp * wg, wg)], tg_o.at[p, blk], 7, tp).start()
+    for tb in other_blk:
+        for tp in [p] + in_plane:
+            to_plane(tg_a.at[:, :, columns(tp * wg, wg)], tg_o.at[p, blk], 7, tp, tb).start()
+    pltpu.make_async_copy(
+        tg_a.at[:, :, columns(p * wg, wg)], tg_o.at[p, blk], p_r.at[7]).start()
     send_act(1)
     arrived(parts_a, a_r.at[6])
     part_b[...] = jnp.sum(parts_a[...], axis=0)
@@ -175,7 +184,7 @@
             qgf[row:row + qtok, :] = qg_o[q, e].astype(f32)
             for b in range(nblk):
                 row = ((e * PLANE + q) * nblk + b) * tok
-                gf[row:row + tok, :] = tg_o[q, e * nblk + b].astype(f32)
+                gf[row:row + tok, :] = tg_o[q, b, e].astype(f32)
     turned = jnp.dot(gf[...].astype(bf), gb_v[...], preferred_element_type=f32)
     grad[...] = turned.astype(bf).astype(f32)
     qgrad = jnp.dot(
@@ -301,7 +310,7 @@
         arrived(qa_o.at[h, p, 0:groups - 1], a_s.at[h])
         arrived(ta_o.at[h, p, 0:column - 1], a_s.at[2 + h])
     arrived(qg_a.at[0:groups - 1], a_s.at[4])
-    arrived(tg_a.at[0:column - 1], a_s.at[5])
+    arrived(tg_a.at[0:groups - 1], a_s.at[5])
     arrived(parts_a.at[0:column - 1], a_s.at[6])
     arrived(slots_a, r_r.at[0])
     red[...] = jnp.sum(slots_a[...], axis=0)
@@ -339,8 +348,8 @@
             vmem(eig.shape, f32), vmem(act_basis.shape, bf), vmem(grad_basis.shape, bf),
             vmem((HALVES, PLANE, column, tok, wh), bf),
             vmem((HALVES, PLANE, groups, qtok, wh), bf),
-            vmem((column, tok, PLANE * wg), bf), vmem((groups, qtok, PLANE * wg), bf),
-            vmem((PLANE, column, tok, wg), bf), vmem((PLANE, groups, qtok, wg), bf),
+            vmem((groups, tok, PLANE * wg), bf), vmem((groups, qtok, PLANE * wg), bf),
+            vmem((PLANE, nblk, groups, tok, wg), bf), vmem((PLANE, groups, qtok, wg), bf),
             vmem((8, 128), f32), vmem((column, 8, 128), f32),
             vmem((8, 128), f32), vmem((PLANE, 8, 128), f32),
             vmem((tokens, wh), f32), vmem((tokens, wg), f32),
@@ -351,7 +360,7 @@
             vmem((QUERIES, tokens, 128), f32), vmem((tokens, 128), f32),
             vmem((ndp, EX_DP, QUERIES), f32), vmem((column, PLANE, EX_DP, QUERIES), f32),
             vmem((PLANE, EX_DP, QUERIES), f32), vmem((PLANE, EX_DP, QUERIES), f32),
-            dma((3,)), dma((7,)), dma((7,)), dma((32,)), dma((20,)),
+            dma((3,)), dma((7,)), dma((7,)), dma((17 + PLANE * (nblk + 1),)), dma((20,)),
             dma((2,)), dma((2,)),
         ],
         compiler_params=pltpu.CompilerParams(

time: 48.4 us -> 47.2 us (0.975)
  Pallas kernels: 47 us -> 45.8 us
    pallas_call x1, Pallas kernels: 47 us -> 45.8 us  [shards_square(): pl.pallas_call(functools.partial(kernel, groups, nblk), out_shape=jax.Sha...]
where the time goes in v6:
time: 47.2 us; the launch traced here: 47 us
  Pallas kernels  45.8 us (97%)
  local copies, waits for them, and re-layouts  1.24 us (3%)
    pallas_call x1, Pallas kernels, shards_square(): pl.pallas_call(functools.partial(kernel, groups, nblk), out_shape=jax.Sha...  45.8 us
    unnamed x1, local copies, waits for them, and re-layouts  1.24 us

profile of v6, /device:TPU:0, one launch (start us, length us, event | category | flops | bytes accessed | tf_op | source)
XLA Modules:
  0.0 47.0 jit_solution(8176803186333261745)
XLA Ops:
  0.0 45.8 %influence.1 = f32[2,16]{1,0:T(2,128)} custom-call(bf16[4,4096]{1,0:T(4,128)(2,1)} %ta.1, bf16[4,8192]{1,0:T(4,128)(2,1)} %tg.1, bf16[4,2048]{1,0:T(4,128)(2,1)} %qa.1, bf16[4,8192]{1,0:T(4,128)(2,1)} %qg.1, bf16[2048,512]{1,0:T(8,128)(2,1)} %act_basis.1, bf16[512,512]{1,0:T(8,128)(2,1)} %grad_basis.1, f32[2048,512]{1,0:T(8,128)} %eig.1, s32[1,64]{1,0:T(1,128)} %bitcast.2, ...), custom_call_target="tpu_custom_call" | custom-call | tf_op jit(solution)/shard_map/influence/pallas_call | solution.py:342
  45.8 1.2 %copy.11 = f32[2,16]{1,0:T(2,128)} copy(f32[2,16]{1,0:T(2,128)} %influence.1) | data formatting | bytes 256
